TPU v7x, 256 devices: a whole 4x4x8 slice. The times are simulated.
256 devices in a mesh: group: 16 (over x, y), delay: 16 (over z, core).
Axes of the slice: x: 4, y: 4, z: 8, core: 2. Of those that a mesh axis runs over, the one named last changes fastest.
Arguments:
- retarded: bfloat16 [16, 256, 3, 256, 256], P('delay', 'group'), may hold values from -0.0234375 to 0.0234375
- block_row: int32 [16, 256, 3], P('delay', 'group'), may hold values from 0 to 3, as said below
- block_count: int32 [16, 256], P('delay', 'group'), may hold values from 1 to 3, as said below
- send_pick: int32 [16, 16, 16], P('delay'), may hold values from 0 to 3
- history: bfloat16 [16, 16384, 128], P('delay', 'group'), may hold values from -6 to 6
- incident: bfloat16 [4, 16384, 128], P(None, 'group'), may hold values from -6 to 6
- self_block: bfloat16 [16384, 1024], P('group'), may hold values from -0.1875 to 0.1875
- sheet_diag: float32 [16384], P('group'), may hold values from 1 to 1.6
Outputs:
- currents: bfloat16 [4, 16384, 128], P(None, 'group')
Inputs may be any that keep to these rules, and one draw needn't show every extreme that they name: `block_row`: the live list places of one section, reading group and source group name distinct row blocks. `block_count`: list places at or beyond the count are ignored.
All inputs are finite; a program needn't handle non-finite values.
Results may differ from a plain program's by a relative error of at most 0.0085.
Values may be sent and summed in bfloat16 or wider, within the bound.
A program may use at most 128 MiB of HBM per device.

v0:
```python
import jax
import jax.numpy as jnp
from jax import lax
from jax.sharding import PartitionSpec as P

STEPS = 4
ITERS = 3


def passed_along(block, axis, distance):
    devices = range(lax.axis_size(axis))
    route = [(i - distance, i) for i in devices if i - distance in devices]
    return lax.ppermute(block, axis, route)


def local(retarded, block_row, block_count, send_pick, history, incident, self_block, sheet_diag):
    group_index = lax.axis_index("group")
    delay_index = lax.axis_index("delay")
    weights = retarded[0]
    row_list = block_row[0]
    live_count = block_count[0]
    picks = send_pick[0]
    history_now = history[0]
    group_rows, columns = history_now.shape
    block_size = weights.shape[-1]
    group_blocks = group_rows // block_size
    list_depth = weights.shape[1]
    block_ids = jnp.arange(group_blocks, dtype=jnp.int32)
    places = jnp.arange(list_depth, dtype=jnp.int32)
    select = (
        (row_list[:, :, None] == block_ids[None, None, :])
        & (places[None, :, None] < live_count[:, None, None])
    ).astype(jnp.float32)
    send_row = lax.dynamic_index_in_dim(picks, group_index, 0, keepdims=False)
    diagonal = sheet_diag[:, None]
    results = []
    for time_step in range(STEPS):
        onehot = (send_row[:, None] == block_ids[None, :]).astype(jnp.bfloat16)
        stacked = jnp.einsum(
            "rb,bic->ric",
            onehot,
            history_now.reshape(group_blocks, block_size, columns),
            preferred_element_type=jnp.float32,
        ).astype(jnp.bfloat16)
        blocks = lax.all_to_all(stacked, "group", split_axis=0, concat_axis=0, tiled=True)
        terms = jnp.einsum("hlij,hjc->hlic", weights, blocks, preferred_element_type=jnp.float32)
        summed = jnp.einsum("hlr,hlic->ric", select, terms, precision=lax.Precision.HIGHEST)
        partial_value = summed.reshape(group_blocks * block_size, blocks.shape[-1])
        total_field = lax.psum(partial_value, "delay")
        driving = incident[time_step].astype(jnp.float32) - total_field
        iterate = driving / diagonal
        for sweep in range(ITERS):
            coupled = jnp.dot(
                self_block, iterate.astype(jnp.bfloat16), preferred_element_type=jnp.float32
            )
            iterate = (driving - coupled) / diagonal
        current = iterate.astype(jnp.bfloat16)
        results.append(current)
        if time_step + 1 < STEPS:
            shifted = passed_along(history_now, "delay", 1)
            history_now = jnp.where(delay_index == 0, current, shifted)
    return jnp.stack(results)


def solution(mesh):
    placed = (
        P("delay", "group", None, None, None),
        P("delay", "group", None),
        P("delay", "group"),
        P("delay", None, None),
        P("delay", "group", None),
        P(None, "group", None),
        P("group", None),
        P("group"),
    )
    return jax.shard_map(
        local, mesh=mesh, in_specs=placed, out_specs=P(None, "group", None), check_vma=False
    )
```

profile of v0, /device:TPU:33, one launch (start us, length us, event | category | flops | bytes accessed | tf_op | source)
XLA Modules:
  0.0 622.6 jit_solution(8567356814555612125)
XLA Ops:
  7.4 1.4 fusion.77
  8.8 1.2 copy.82
  10.1 6.8 %all-to-all-start = ((bf16[16,256,128]{2,1,0:T(8,128)(2,1)}), bf16[16,256,128]{2,1,0:T(8,128)(2,1)S(1)}, u32[]{:S(2)}, u32[]{:S(2)}) async-start(bf16[16,256,128]{2,1,0:T(8,128)(2,1)} %copy.82), calls=%async_computation | async-start | bytes 2097152 | tf_op jit(solution)/shard_map/all_to_all | solution.py:45
  18.2 14.1 %all-to-all-done = bf16[16,256,128]{2,1,0:T(8,128)(2,1)S(1)} async-done(((bf16[16,256,128]{2,1,0:T(8,128)(2,1)}), bf16[16,256,128]{2,1,0:T(8,128)(2,1)S(1)}, u32[]{:S(2)}, u32[]{:S(2)}) %all-to-all-start) | async-done | bytes 1048608 | tf_op jit(solution)/shard_map/all_to_all | solution.py:45
  32.3 7.7 %fusion.14 = f32[16,128,3,256]{3,1,2,0:T(8,128)} fusion(bf16[1,16,3,256,256]{4,3,2,1,0:T(8,128)(2,1)} %param.8, bf16[16,256,128]{2,1,0:T(8,128)(2,1)S(1)} %all-to-all-done), kind=kOutput, calls=%fused_computation.14 | convolution fusion | flops 805306368 | bytes 13631488 | tf_op jit(solution)/shard_map/hlij,hjc->hlic/dot_general | solution.py:46
  40.0 6.6 %copy.32 = f32[16,128,3,256]{1,0,2,3:T(8,128)} copy(f32[16,128,3,256]{3,1,2,0:T(8,128)} %fusion.14) | data formatting | bytes 12582912 | tf_op jit(solution)/shard_map/hlij,hjc->hlic/dot_general | solution.py:46
  46.6 5.1 fusion.25
  52.9 6.6 %collective-permute-start = (bf16[1024,128]{0,1:T(8,128)(2,1)S(1)}, bf16[1024,128]{0,1:T(8,128)(2,1)}, u32[]{:S(2)}, u32[]{:S(2)}) collective-permute-start(bf16[1024,128]{0,1:T(8,128)(2,1)S(1)} %bitcast.278), channel_id=1, source_target_pairs={{0,1},{1,2},{2,3},{3,4},{4,5},{5,6},{6,7},{7,8},{8,9},{9,10},{10,1... | collective-permute-start | bytes 786440 | tf_op jit(solution)/shard_map/ppermute | solution.py:13
  59.5 1.3 fusion.105
  61.7 99.9 %all-reduce.5.cloned.1.call-done = f32[1024,128]{0,1:T(8,128)} async-done(((f32[1024,128]{0,1:T(8,128)}), f32[1024,128]{0,1:T(8,128)}) %all-reduce.5.cloned.1.call-update) | async-done | bytes 524304 | tf_op jit(solution)/shard_map/psum | solution.py:49
  161.6 4.0 fusion.62
  165.6 2.9 broadcast_select_fusion.2
  170.3 22.8 %all_to_all.20 = bf16[16,256,128]{2,1,0:T(8,128)(2,1)S(1)} all-to-all(bf16[16,256,128]{2,1,0:T(8,128)(2,1)S(1)} %copy.81), channel_id=1, replica_groups=mesh['group'=16,'delay'=16] {'group'}, dimensions={0} | all-to-all | bytes 2097152 | tf_op jit(solution)/shard_map/all_to_all | solution.py:45
  193.1 5.0 fusion.16
  198.1 5.8 fusion.4
  205.0 6.3 %collective-permute-start.1 = (bf16[1024,128]{0,1:T(8,128)(2,1)S(1)}, bf16[1024,128]{0,1:T(8,128)(2,1)}, u32[]{:S(2)}, u32[]{:S(2)}) collective-permute-start(bf16[1024,128]{0,1:T(8,128)(2,1)S(1)} %copy-done.6), channel_id=1, source_target_pairs={{0,1},{1,2},{2,3},{3,4},{4,5},{5,6},{6,7},{7,8},{8,9},{9,10},{10,1... | collective-permute-start | bytes 786440 | tf_op jit(solution)/shard_map/ppermute | solution.py:13
  211.3 100.6 %all-reduce.7.cloned.1.call-done = f32[1024,128]{0,1:T(8,128)} async-done(((f32[1024,128]{0,1:T(8,128)}), f32[1024,128]{0,1:T(8,128)}) %all-reduce.7.cloned.1.call-update) | async-done | bytes 524304 | tf_op jit(solution)/shard_map/psum | solution.py:49
  311.9 3.0 fusion.59
  314.8 1.9 fusion.58
  319.6 22.5 %all_to_all.21 = bf16[16,256,128]{2,1,0:T(8,128)(2,1)S(1)} all-to-all(bf16[16,256,128]{2,1,0:T(8,128)(2,1)S(1)} %copy.80), channel_id=1, replica_groups=mesh['group'=16,'delay'=16] {'group'}, dimensions={0} | all-to-all | bytes 2097152 | tf_op jit(solution)/shard_map/all_to_all | solution.py:45
  342.1 5.0 fusion.19
  347.1 5.8 fusion.2
  354.0 6.3 %collective-permute-start.2 = (bf16[1024,128]{0,1:T(8,128)(2,1)S(1)}, bf16[1024,128]{0,1:T(8,128)(2,1)S(1)}, u32[]{:S(2)}, u32[]{:S(2)}) collective-permute-start(bf16[1024,128]{0,1:T(8,128)(2,1)S(1)} %broadcast_select_fusion.1), channel_id=1, source_target_pairs={{0,1},{1,2},{2,3},{3,4},{4,5},{5,6},{6,7},{7,8},{8,9},{9,10},{10,1... | collective-permute-start | bytes 786440 | tf_op jit(solution)/shard_map/ppermute | solution.py:13
  360.3 100.4 %all-reduce.9.cloned.1.call-done = f32[1024,128]{0,1:T(8,128)} async-done(((f32[1024,128]{0,1:T(8,128)}), f32[1024,128]{0,1:T(8,128)}) %all-reduce.9.cloned.1.call-update) | async-done | bytes 524304 | tf_op jit(solution)/shard_map/psum | solution.py:49
  460.7 3.7 fusion.56
  464.3 2.0 fusion.55
  468.2 22.5 %all_to_all.22 = bf16[16,256,128]{2,1,0:T(8,128)(2,1)S(1)} all-to-all(bf16[16,256,128]{2,1,0:T(8,128)(2,1)S(1)} %copy.79), channel_id=1, replica_groups=mesh['group'=16,'delay'=16] {'group'}, dimensions={0} | all-to-all | bytes 2097152 | tf_op jit(solution)/shard_map/all_to_all | solution.py:45
  490.7 5.0 fusion.22
  495.7 5.8 fusion
  502.6 106.9 %all-reduce.11.cloned.1.call-done = f32[1024,128]{0,1:T(8,128)} async-done(((f32[1024,128]{0,1:T(8,128)}), f32[1024,128]{0,1:T(8,128)}) %all-reduce.11.cloned.1.call-update) | async-done | bytes 524304 | tf_op jit(solution)/shard_map/psum | solution.py:49
  609.5 3.0 fusion.53
  614.5 1.3 copy.28
  (58 shorter events, 16.2 us)
Async XLA Ops:
  6.5 155.0 %copy-start = (bf16[1024,1024]{1,0:T(8,128)(2,1)S(1)}, bf16[1024,1024]{1,0:T(8,128)(2,1)}, u32[]{:S(2)}) copy-start(bf16[1024,1024]{1,0:T(8,128)(2,1)} %param.14) | copy-start | bytes 6291460
  10.1 22.3 %all-to-all-start = ((bf16[16,256,128]{2,1,0:T(8,128)(2,1)}), bf16[16,256,128]{2,1,0:T(8,128)(2,1)S(1)}, u32[]{:S(2)}, u32[]{:S(2)}) async-start(bf16[16,256,128]{2,1,0:T(8,128)(2,1)} %copy.82), calls=%async_computation | async-start | bytes 2097152 | tf_op jit(solution)/shard_map/all_to_all | solution.py:45
  16.8 144.7 %all-reduce.5.cloned.1.call-start = ((), (), s32[]{:S(2)}) async-start(), calls=%async_computation.4 | async-start | bytes 1048576 | tf_op jit(solution)/shard_map/psum | solution.py:49
  46.6 6.2 copy-start.1
  46.6 115.0 %copy-start.8 = (f32[1024]{0:T(1024)S(1)}, f32[1024]{0:T(1024)}, u32[]{:S(2)}) copy-start(f32[1024]{0:T(1024)} %param.15) | copy-start | bytes 12292
  52.7 259.1 %all-reduce.7.cloned.1.call-start = ((), (), s32[]{:S(2)}) async-start(), calls=%async_computation.5 | async-start | bytes 1048576 | tf_op jit(solution)/shard_map/psum | solution.py:49
  52.9 112.6 %collective-permute-start = (bf16[1024,128]{0,1:T(8,128)(2,1)S(1)}, bf16[1024,128]{0,1:T(8,128)(2,1)}, u32[]{:S(2)}, u32[]{:S(2)}) collective-permute-start(bf16[1024,128]{0,1:T(8,128)(2,1)S(1)} %bitcast.278), channel_id=1, source_target_pairs={{0,1},{1,2},{2,3},{3,4},{4,5},{5,6},{6,7},{7,8},{8,9},{9,10},{10,1... | collective-permute-start | bytes 786440 | tf_op jit(solution)/shard_map/ppermute | solution.py:13
  168.4 0.7 copy-start.5
  198.1 6.9 %copy-start.6 = (bf16[1024,128]{0,1:T(8,128)(2,1)S(1)}, bf16[1024,128]{0,1:T(8,128)(2,1)}, u32[]{:S(2)}) copy-start(bf16[1024,128]{0,1:T(8,128)(2,1)} %copy-done.5) | copy-start | bytes 786436
  204.8 255.9 %all-reduce.9.cloned.1.call-start = ((), (), s32[]{:S(2)}) async-start(), calls=%async_computation.6 | async-start | bytes 1048576 | tf_op jit(solution)/shard_map/psum | solution.py:49
  205.0 111.7 %collective-permute-start.1 = (bf16[1024,128]{0,1:T(8,128)(2,1)S(1)}, bf16[1024,128]{0,1:T(8,128)(2,1)}, u32[]{:S(2)}, u32[]{:S(2)}) collective-permute-start(bf16[1024,128]{0,1:T(8,128)(2,1)S(1)} %copy-done.6), channel_id=1, source_target_pairs={{0,1},{1,2},{2,3},{3,4},{4,5},{5,6},{6,7},{7,8},{8,9},{9,10},{10,1... | collective-permute-start | bytes 786440 | tf_op jit(solution)/shard_map/ppermute | solution.py:13
  316.7 0.7 copy-start.2
  353.8 255.8 %all-reduce.11.cloned.1.call-start = ((), (), s32[]{:S(2)}) async-start(), calls=%async_computation.7 | async-start | bytes 1048576 | tf_op jit(solution)/shard_map/psum | solution.py:49
  354.0 112.3 %collective-permute-start.2 = (bf16[1024,128]{0,1:T(8,128)(2,1)S(1)}, bf16[1024,128]{0,1:T(8,128)(2,1)S(1)}, u32[]{:S(2)}, u32[]{:S(2)}) collective-permute-start(bf16[1024,128]{0,1:T(8,128)(2,1)S(1)} %broadcast_select_fusion.1), channel_id=1, source_target_pairs={{0,1},{1,2},{2,3},{3,4},{4,5},{5,6},{6,7},{7,8},{8,9},{9,10},{10,1... | collective-permute-start | bytes 786440 | tf_op jit(solution)/shard_map/ppermute | solution.py:13
  466.3 0.7 copy-start.4
  502.6 110.8 %copy-start.3 = (bf16[1024,128]{0,1:T(8,128)(2,1)S(1)}, bf16[1024,128]{0,1:T(8,128)(2,1)}, u32[]{:S(2)}) copy-start(bf16[1024,128]{0,1:T(8,128)(2,1)} %copy-done.2) | copy-start | bytes 786436
  609.5 3.0 copy-start.7
Sparse Core Ops, SparseCore 0:
  52.8 108.6 all-reduce.4
  204.9 106.9 all-reduce.6
  353.9 106.7 all-reduce.8
  502.5 106.9 all-reduce.10
where the time goes:
time: 634 us; the launch traced here: 623 us
  waiting for transfers between devices  422 us (67%)
  matrix products  69 us (11%)
  blocking collectives  67.7 us (11%)
  starting transfers between devices  26 us (4%)
  local copies, waits for them, and re-layouts  21.3 us (3%)
  between operations  13.7 us (2%)
    psum x4, waiting for transfers between devices, local(): total_field = lax.psum(partial_value, 'delay')  408 us
    all_to_all x3, blocking collectives, local(): lax.all_to_all(stacked, 'group', split_axis=0, concat_axis=0, tiled=True)  67.7 us
    dot_general x4, matrix products, local(): jnp.einsum('hlij,hjc->hlic', weights, blocks, preferred_element_type=jnp....  22.6 us
    dot_general x4, matrix products, local(): jnp.einsum('hlr,hlic->ric', select, terms, precision=lax.Precision.HIGHEST)  22.4 us
    dot_general x8, matrix products, local(): jnp.dot(self_block, iterate.astype(jnp.bfloat16), preferred_element_type=...  21.1 us
    ppermute x3, starting transfers between devices, passed_along(): return lax.ppermute(block, axis, route)  19.1 us
    all_to_all x1, waiting for transfers between devices, local(): lax.all_to_all(stacked, 'group', split_axis=0, concat_axis=0, tiled=True)  14.1 us
  transfers between devices with their start and end apart: 8, of which 5 were waited for; matrix products, arithmetic and copies ran while one was open for 3% of the time, Pallas kernels for 0%

commit v1 on v0

v1 whole, which is shorter than its diff:
```python
import jax
import jax.numpy as jnp
from jax import lax
from jax.experimental import pallas as pl
from jax.experimental.pallas import tpu as pltpu
from jax.sharding import PartitionSpec as P

STEPS = 4
ITERS = 3
SIDE = 4
GROUPS = 16
DELAYS = 16
CHIPS = 8
BLK = 256
ROWS = 1024
COLS = 128
PLACES = 3
MESH = pl.DeviceIdType.MESH
OFFSETS = sorted(
    [(dx, dy) for dx in range(SIDE) for dy in range(SIDE) if (dx, dy) != (0, 0)],
    key=lambda o: -(min(o[0], SIDE - o[0]) + min(o[1], SIDE - o[1])),
)


def kernel(
    row_ref, count_ref, pick_ref, weights_hbm, history_hbm, incident_hbm, self_hbm, diag_ref, out_hbm,
    weights, dense, self_block, incident, held, source, staged, blocks, total, rdiag, driving, iterate,
    partial_out, pair_in, chip_in, currents,
    local_sem, block_send, block_recv, shift_send, shift_recv, pair_send, pair_recv,
    chip_send, chip_recv, cast_send, cast_recv, fan_send, fan_recv, out_sem,
):
    g = lax.axis_index("group")
    d = lax.axis_index("delay")
    x, y = g // SIDE, g % SIDE
    chip, core = d // 2, d % 2
    first = d == 0

    def peer(dx, dy):
        return ((x + dx) % SIDE) * SIDE + (y + dy) % SIDE

    local = [
        pltpu.make_async_copy(history_hbm, held.at[0], local_sem.at[0]),
        pltpu.make_async_copy(weights_hbm, weights.at[pl.ds(0, GROUPS * PLACES)], local_sem.at[1]),
        pltpu.make_async_copy(self_hbm, self_block, local_sem.at[2]),
        pltpu.make_async_copy(incident_hbm, incident, local_sem.at[3]),
    ]
    for copy in local:
        copy.start()

    barrier = pltpu.get_barrier_semaphore()
    for dx, dy in OFFSETS:
        pl.semaphore_signal(barrier, inc=1, device_id=(peer(dx, dy), d), device_id_type=MESH)

    @pl.when(first)
    def _():
        for z in range(1, CHIPS):
            pl.semaphore_signal(barrier, inc=1, device_id=(g, 2 * z), device_id_type=MESH)
        pl.semaphore_signal(barrier, inc=1, device_id=(g, 1), device_id_type=MESH)
        pl.semaphore_wait(barrier, 15 + CHIPS)

    @pl.when(jnp.logical_and(core == 0, d > 0))
    def _():
        for other in (0, d - 1, d + 1):
            pl.semaphore_signal(barrier, inc=1, device_id=(g, other), device_id_type=MESH)
        pl.semaphore_wait(barrier, 15 + 3)

    @pl.when(jnp.logical_and(core == 1, d < DELAYS - 1))
    def _():
        for other in (d - 1, d + 1):
            pl.semaphore_signal(barrier, inc=1, device_id=(g, other), device_id_type=MESH)
        pl.semaphore_wait(barrier, 15 + 2)

    @pl.when(d == DELAYS - 1)
    def _():
        pl.semaphore_signal(barrier, inc=1, device_id=(g, d - 1), device_id_type=MESH)
        pl.semaphore_wait(barrier, 15 + 1)

    def shift(n):
        return pltpu.make_async_remote_copy(
            src_ref=held.at[n], dst_ref=held.at[n + 1], send_sem=shift_send.at[n], recv_sem=shift_recv.at[n + 1],
            device_id=(g, d + 1), device_id_type=MESH,
        )

    def block_copy(n, dx, dy):
        h = peer(dx, dy)
        return pltpu.make_async_remote_copy(
            src_ref=staged.at[n, h], dst_ref=blocks.at[n, x, y],
            send_sem=block_send.at[n, h], recv_sem=block_recv.at[n, g],
            device_id=(h, d), device_id_type=MESH,
        )

    def block_arrival(n, hx, hy):
        return pltpu.make_async_remote_copy(
            src_ref=staged.at[n, 0], dst_ref=blocks.at[n, hx, hy],
            send_sem=block_send.at[n, 0], recv_sem=block_recv.at[n, hx * SIDE + hy],
            device_id=(peer(1, 0), d), device_id_type=MESH,
        )

    def send_blocks(n):
        source[...] = held[n]
        for dx, dy in OFFSETS:
            h = peer(dx, dy)
            staged[n, h] = source[pick_ref[g, h]]
            block_copy(n, dx, dy).start()
        blocks[n, x, y] = source[pick_ref[g, g]]

        @pl.when(jnp.logical_and(n < STEPS - 1, d < DELAYS - 1))
        def _():
            shift(n).start()

    def pair(n):
        return pltpu.make_async_remote_copy(
            src_ref=partial_out.at[n], dst_ref=pair_in.at[n], send_sem=pair_send.at[n], recv_sem=pair_recv.at[n],
            device_id=(g, d - 1), device_id_type=MESH,
        )

    def to_first(n):
        return pltpu.make_async_remote_copy(
            src_ref=partial_out.at[n], dst_ref=chip_in.at[n, chip], send_sem=chip_send.at[n],
            recv_sem=chip_recv.at[n, chip], device_id=(g, 0), device_id_type=MESH,
        )

    def from_chip(n, z):
        return pltpu.make_async_remote_copy(
            src_ref=partial_out.at[n], dst_ref=chip_in.at[n, z], send_sem=chip_send.at[n],
            recv_sem=chip_recv.at[n, z], device_id=(g, 2), device_id_type=MESH,
        )

    def cast(n, z):
        return pltpu.make_async_remote_copy(
            src_ref=currents.at[n], dst_ref=currents.at[n], send_sem=cast_send.at[n, z], recv_sem=cast_recv.at[n],
            device_id=(g, 2 * z), device_id_type=MESH,
        )

    def fan(n):
        return pltpu.make_async_remote_copy(
            src_ref=currents.at[n], dst_ref=currents.at[n], send_sem=fan_send.at[n], recv_sem=fan_recv.at[n],
            device_id=(g, d + 1), device_id_type=MESH,
        )

    def store(n):
        return pltpu.make_async_copy(currents.at[n], out_hbm.at[n], out_sem.at[n])

    local[0].wait()
    send_blocks(0)

    weights[GROUPS * PLACES] = jnp.zeros((BLK, BLK), weights.dtype)
    for i in range(SIDE * 2):
        rows = jnp.broadcast_to(diag_ref[i : i + 1, :], (COLS, COLS))
        rdiag[pl.ds(i * COLS, COLS), :] = 1.0 / jnp.transpose(rows)
    local[1].wait()

    def spread(hx, carry):
        for hy in range(SIDE):
            h = hx * SIDE + hy
            for r in range(SIDE):
                place = jnp.int32(GROUPS * PLACES)
                for l in range(PLACES):
                    hit = jnp.logical_and(row_ref[h, l] == r, l < count_ref[h])
                    place = jnp.where(hit, h * PLACES + l, place)
                dense[hx, pl.ds(r * BLK, BLK), pl.ds(hy * BLK, BLK)] = weights[place]
        return carry

    lax.fori_loop(0, SIDE, spread, 0)
    local[2].wait()
    local[3].wait()

    def step(n, carry):
        def chunk(c, carry):
            hx = (x + c) % SIDE
            for hy in range(SIDE):
                @pl.when(jnp.logical_not(jnp.logical_and(hx == x, hy == y)))
                def _():
                    block_arrival(n, hx, hy).wait_recv()

            @pl.when(jnp.logical_and(c == SIDE - 1, jnp.logical_and(d > 0, n < STEPS - 1)))
            def _():
                shift_in = pltpu.make_async_remote_copy(
                    src_ref=held.at[n], dst_ref=held.at[n + 1], send_sem=shift_send.at[n],
                    recv_sem=shift_recv.at[n + 1], device_id=(g, d - 1), device_id_type=MESH,
                )
                shift_in.wait_recv()
                send_blocks(n + 1)

            value = jnp.dot(
                dense[hx], blocks[n, hx].reshape(ROWS, COLS), preferred_element_type=jnp.float32
            )

            @pl.when(c == 0)
            def _():
                total[...] = value

            @pl.when(c > 0)
            def _():
                total[...] += value

            return carry

        lax.fori_loop(0, SIDE, chunk, 0)

        @pl.when(core == 1)
        def _():
            partial_out[n] = total[...].astype(jnp.bfloat16)
            pair(n).start()

        @pl.when(jnp.logical_and(core == 0, d > 0))
        def _():
            from_pair(n).wait_recv()
            partial_out[n] = (total[...] + pair_in[n].astype(jnp.float32)).astype(jnp.bfloat16)
            to_first(n).start()

        @pl.when(first)
        def _():
            from_pair(n).wait_recv()
            value = incident[n].astype(jnp.float32) - total[...] - pair_in[n].astype(jnp.float32)
            driving[...] = value

            def gather(z, carry):
                from_chip(n, z).wait_recv()
                driving[...] -= chip_in[n, z].astype(jnp.float32)
                return carry

            lax.fori_loop(1, CHIPS, gather, 0)
            iterate[...] = driving[...] * rdiag[...]

            def sweep(k, carry):
                coupled = jnp.dot(
                    self_block[...], iterate[...].astype(jnp.bfloat16), preferred_element_type=jnp.float32
                )
                iterate[...] = (driving[...] - coupled) * rdiag[...]
                return carry

            lax.fori_loop(0, ITERS, sweep, 0)
            current = iterate[...].astype(jnp.bfloat16)
            currents[n] = current

            @pl.when(n < STEPS - 1)
            def _():
                held[n + 1] = current.reshape(SIDE, BLK, COLS)
                send_blocks(n + 1)

            for z in (4, 3, 5, 2, 6, 1, 7):
                cast(n, z).start()
            fan(n).start()
            store(n).start()

        return carry

    def from_pair(n):
        return pltpu.make_async_remote_copy(
            src_ref=partial_out.at[n], dst_ref=pair_in.at[n], send_sem=pair_send.at[n], recv_sem=pair_recv.at[n],
            device_id=(g, d + 1), device_id_type=MESH,
        )

    lax.fori_loop(0, STEPS, step, 0)

    def finish(n, carry):
        @pl.when(jnp.logical_and(core == 0, d > 0))
        def _():
            cast_in = pltpu.make_async_remote_copy(
                src_ref=currents.at[n], dst_ref=currents.at[n], send_sem=cast_send.at[n, 0],
                recv_sem=cast_recv.at[n], device_id=(g, 0), device_id_type=MESH,
            )
            cast_in.wait_recv()
            fan(n).start()
            store(n).start()

        @pl.when(core == 1)
        def _():
            fan_in = pltpu.make_async_remote_copy(
                src_ref=currents.at[n], dst_ref=currents.at[n], send_sem=fan_send.at[n],
                recv_sem=fan_recv.at[n], device_id=(g, d - 1), device_id_type=MESH,
            )
            fan_in.wait_recv()
            store(n).start()

        return carry

    lax.fori_loop(0, STEPS, finish, 0)

    def drain(n, carry):
        for dx, dy in OFFSETS:
            block_copy(n, dx, dy).wait_send()

        @pl.when(jnp.logical_and(n < STEPS - 1, d < DELAYS - 1))
        def _():
            shift(n).wait_send()

        @pl.when(core == 1)
        def _():
            pair(n).wait_send()

        @pl.when(core == 0)
        def _():
            fan(n).wait_send()

        @pl.when(jnp.logical_and(core == 0, d > 0))
        def _():
            to_first(n).wait_send()

        @pl.when(first)
        def _():
            for z in range(1, CHIPS):
                cast(n, z).wait_send()

        store(n).wait()
        return carry

    lax.fori_loop(0, STEPS, drain, 0)


def local(retarded, block_row, block_count, send_pick, history, incident, self_block, sheet_diag):
    smem = pl.BlockSpec(memory_space=pltpu.SMEM)
    vmem = pl.BlockSpec(memory_space=pltpu.VMEM)
    hbm = pl.BlockSpec(memory_space=pl.ANY)
    bf16, f32 = jnp.bfloat16, jnp.float32
    dma = pltpu.SemaphoreType.DMA
    call = pl.pallas_call(
        kernel,
        out_shape=jax.ShapeDtypeStruct((STEPS, ROWS, COLS), bf16),
        in_specs=[smem, smem, smem, hbm, hbm, hbm, hbm, vmem],
        out_specs=hbm,
        scratch_shapes=[
            pltpu.VMEM((GROUPS * PLACES + 1, BLK, BLK), bf16),
            pltpu.VMEM((SIDE, ROWS, ROWS), bf16),
            pltpu.VMEM((ROWS, ROWS), bf16),
            pltpu.VMEM((STEPS, ROWS, COLS), bf16),
            pltpu.VMEM((STEPS, SIDE, BLK, COLS), bf16),
            pltpu.VMEM((SIDE, BLK, COLS), bf16),
            pltpu.VMEM((STEPS, GROUPS, BLK, COLS), bf16),
            pltpu.VMEM((STEPS, SIDE, SIDE, BLK, COLS), bf16),
            pltpu.VMEM((ROWS, COLS), f32),
            pltpu.VMEM((ROWS, COLS), f32),
            pltpu.VMEM((ROWS, COLS), f32),
            pltpu.VMEM((ROWS, COLS), f32),
            pltpu.VMEM((STEPS, ROWS, COLS), bf16),
            pltpu.VMEM((STEPS, ROWS, COLS), bf16),
            pltpu.VMEM((STEPS, CHIPS, ROWS, COLS), bf16),
            pltpu.VMEM((STEPS, ROWS, COLS), bf16),
            dma((4,)),
            dma((STEPS, GROUPS)), dma((STEPS, GROUPS)),
            dma((STEPS,)), dma((STEPS,)),
            dma((STEPS,)), dma((STEPS,)),
            dma((STEPS,)), dma((STEPS, CHIPS)),
            dma((STEPS, CHIPS)), dma((STEPS,)),
            dma((STEPS,)), dma((STEPS,)),
            dma((STEPS,)),
        ],
        compiler_params=pltpu.CompilerParams(
            collective_id=0, has_side_effects=True, vmem_limit_bytes=56 * 2**20
        ),
        cost_estimate=pl.CostEstimate(flops=8 * 10**9, bytes_accessed=12 * 10**6, transcendentals=0),
    )
    return call(
        block_row[0], block_count[0], send_pick[0],
        retarded.reshape(GROUPS * PLACES, BLK, BLK), history.reshape(SIDE, BLK, COLS),
        incident, self_block, sheet_diag.reshape(SIDE * 2, COLS),
    )


def solution(mesh):
    placed = (
        P("delay", "group", None, None, None),
        P("delay", "group", None),
        P("delay", "group"),
        P("delay", None, None),
        P("delay", "group", None),
        P(None, "group", None),
        P("group", None),
        P("group"),
    )
    return jax.shard_map(
        local, mesh=mesh, in_specs=placed, out_specs=P(None, "group", None), check_vma=False
    )
```

time: 634 us -> 119 us (0.19); the launches traced: 623 us -> 119 us
  waiting for transfers between devices: 422 us -> 0 us
  Pallas kernels: 0 us -> 116 us
  matrix products: 69 us -> 0 us
  blocking collectives: 67.7 us -> 0 us
  starting transfers between devices: 26 us -> 0 us
  local copies, waits for them, and re-layouts: 21.3 us -> 3.62 us
  between operations: 13.7 us -> 0.01 us
    psum x4 -> x0, waiting for transfers between devices: 408 us -> none  [local(): total_field = lax.psum(partial_value, 'delay')]
    pallas_call x0 -> x1, Pallas kernels: none -> 116 us  [local(): call(block_row[0], block_count[0], send_pick[0], retarded.reshape(GROUPS...]
    dot_general x20 -> x0, matrix products: 69 us -> none  [the longest x4 22.6 us: local(): jnp.einsum('hlij,hjc->hlic', weights, blocks, preferred_element_type=jnp....]
    all_to_all x3 -> x0, blocking collectives: 67.7 us -> none  [local(): lax.all_to_all(stacked, 'group', split_axis=0, concat_axis=0, tiled=True)]
    ppermute x3 -> x0, starting transfers between devices: 19.1 us -> none  [passed_along(): return lax.ppermute(block, axis, route)]
    all_to_all x1 -> x0, waiting for transfers between devices: 14.1 us -> none  [local(): lax.all_to_all(stacked, 'group', split_axis=0, concat_axis=0, tiled=True)]
    dot_general x6 -> x0, local copies, waits for them, and re-layouts: 8.69 us -> none  [the longest x1 6.6 us: local(): jnp.einsum('hlij,hjc->hlic', weights, blocks, preferred_element_type=jnp....]
    all_to_all x1 -> x0, starting transfers between devices: 6.75 us -> none  [local(): lax.all_to_all(stacked, 'group', split_axis=0, concat_axis=0, tiled=True)]
  transfers between devices with their start and end apart: 8 -> 0, of which waited for: 5 -> 0; matrix products, arithmetic and copies ran while one was open for 3% -> 0% of each run, Pallas kernels for 0% -> 0%
where the time goes in v1:
time: 119 us
  Pallas kernels  116 us (97%)
  local copies, waits for them, and re-layouts  3.62 us (3%)
    pallas_call x1, Pallas kernels, local(): call(block_row[0], block_count[0], send_pick[0], retarded.reshape(GROUPS...  116 us

profile of v1, /device:TPU:33, one launch (start us, length us, event | category | flops | bytes accessed | tf_op | source)
XLA Modules:
  0.0 119.2 jit_solution(12882757561562193586)
XLA Ops:
  0.0 1.4 %copy.10 = s32[1,16,3]{2,1,0:T(8,128)} copy(s32[1,16,3]{1,0,2:T(1,128)} %param.9) | data formatting | bytes 384 | tf_op jit(solution)/shard_map/squeeze | solution.py:355
  1.4 115.6 %shard_map.82 = bf16[4,1024,128]{2,1,0:T(8,128)(2,1)} custom-call(s32[16,3]{1,0:T(8,128)} %bitcast.6, s32[16]{0:T(128)} %bitcast.11, s32[16,16]{1,0:T(8,128)} %bitcast.9, bf16[48,256,256]{2,1,0:T(8,128)(2,1)} %bitcast.7, bf16[4,256,128]{2,1,0:T(8,128)(2,1)} %bitcast.8, bf16[4,1024,128]{2,1,0:T(8,128)(2,1)} %incident_hbm.1, bf16[1024,1024]{1,0:T(8,128)(2,1)} %self_hbm.1, ...), custom_call_target="tpu_custom_call" | custom-call | flops 8000000000 | bytes 12000000 | tf_op jit(solution)/shard_map/pallas_call | solution.py:354
  116.9 2.3 %copy.12 = bf16[4,1024,128]{2,1,0:T(8,128)(2,1)} copy(bf16[4,1024,128]{2,1,0:T(8,128)(2,1)} %shard_map.82) | data formatting | bytes 2097152

commit v2 on v1

v2 whole, which is shorter than its diff:
```python
import jax
import jax.numpy as jnp
from jax import lax
from jax.experimental import pallas as pl
from jax.experimental.pallas import tpu as pltpu
from jax.sharding import PartitionSpec as P

STEPS = 4
SIDE = 4
GROUPS = 16
DELAYS = 16
CHIPS = 8
BLK = 256
ROWS = 1024
COLS = 128
PLACES = 3
MESH = pl.DeviceIdType.MESH
HALF = ROWS // 2
PART = HALF // CHIPS
SLAB = ROWS // CHIPS
OFFSETS = [(dx, dy) for dx in (2, 1, 3, 0) for dy in (2, 1, 3, 0) if (dx, dy) != (0, 0)]


def kernel(
    row_ref, count_ref, pick_ref, weights_hbm, history_hbm, incident_hbm, self_hbm, diag_ref, out_hbm,
    weights, dense, self_block, ratio, power, incident, held, source, staged, blocks, total, rdiag,
    pair_out, pair_in, half_out, half_in, part_out, part_in, chunk_out, chunk_in, first_in, currents,
    local_sem, block_send, block_recv, shift_send, shift_recv, pair_send, pair_recv, half_send, half_recv,
    part_send, part_recv, chunk_send, chunk_recv, first_recv,
    cast_send, cast_recv, fan_send, fan_recv, out_sem, turn_sem,
):
    g = lax.axis_index("group")
    d = lax.axis_index("delay")
    x, y = g // SIDE, g % SIDE
    chip, core = d // 2, d % 2
    first = d == 0

    def peer(dx, dy):
        return ((x + dx) % SIDE) * SIDE + (y + dy) % SIDE

    local = [
        pltpu.make_async_copy(history_hbm, held.at[0], local_sem.at[0]),
        pltpu.make_async_copy(weights_hbm, weights.at[pl.ds(0, GROUPS * PLACES)], local_sem.at[1]),
        pltpu.make_async_copy(self_hbm, self_block, local_sem.at[2]),
        pltpu.make_async_copy(incident_hbm, incident, local_sem.at[3]),
    ]
    for copy in local:
        copy.start()

    barrier = pltpu.get_barrier_semaphore()
    for dx, dy in OFFSETS:
        pl.semaphore_signal(barrier, inc=1, device_id=(peer(dx, dy), d), device_id_type=MESH)

    @pl.when(first)
    def _():
        for other in range(1, DELAYS):
            pl.semaphore_signal(barrier, inc=1, device_id=(g, other), device_id_type=MESH)

    @pl.when(d == 1)
    def _():
        for other in (0, 2):
            pl.semaphore_signal(barrier, inc=1, device_id=(g, other), device_id_type=MESH)

    @pl.when(d > 1)
    def _():
        pl.semaphore_signal(barrier, inc=1, device_id=(g, 0), device_id_type=MESH)
        pl.semaphore_signal(barrier, inc=1, device_id=(g, d - 1), device_id_type=MESH)

        @pl.when(d < DELAYS - 1)
        def _():
            pl.semaphore_signal(barrier, inc=1, device_id=(g, d + 1), device_id_type=MESH)

        for j in range(1, CHIPS):
            @pl.when(j != chip)
            def _():
                pl.semaphore_signal(barrier, inc=1, device_id=(g, 2 * j + core), device_id_type=MESH)

    def enter():
        greeted = jnp.where(d == 0, 15, jnp.where(d == 1, 2, jnp.where(d == DELAYS - 1, 8, 9)))
        pl.semaphore_wait(barrier, 15 + greeted)

    def shift(n):
        return pltpu.make_async_remote_copy(
            src_ref=held.at[n], dst_ref=held.at[n + 1], send_sem=shift_send.at[n], recv_sem=shift_recv.at[n + 1],
            device_id=(g, d + 1), device_id_type=MESH,
        )

    def block_copy(n, dx, dy):
        h = peer(dx, dy)
        return pltpu.make_async_remote_copy(
            src_ref=staged.at[n, h], dst_ref=blocks.at[n, x, y],
            send_sem=block_send.at[n, h], recv_sem=block_recv.at[n, g],
            device_id=(h, d), device_id_type=MESH,
        )

    def block_arrival(n, hx, hy):
        return pltpu.make_async_remote_copy(
            src_ref=staged.at[n, 0], dst_ref=blocks.at[n, hx, hy],
            send_sem=block_send.at[n, 0], recv_sem=block_recv.at[n, hx * SIDE + hy],
            device_id=(peer(1, 0), d), device_id_type=MESH,
        )

    def pack(n):
        source[...] = held[n]
        for dx, dy in OFFSETS:
            h = peer(dx, dy)
            staged[n, h] = source[pick_ref[g, h]]
        blocks[n, x, y] = source[pick_ref[g, g]]

    def start_shift(n):
        @pl.when(jnp.logical_and(n < STEPS - 1, jnp.logical_and(d >= n, d < DELAYS - 1)))
        def _():
            shift(n).start()

    def send_blocks(n):
        source[...] = held[n]
        for dx, dy in OFFSETS:
            h = peer(dx, dy)
            staged[n, h] = source[pick_ref[g, h]]
            block_copy(n, dx, dy).start()
        blocks[n, x, y] = source[pick_ref[g, g]]

    def pair(n, target):
        return pltpu.make_async_remote_copy(
            src_ref=pair_out.at[n], dst_ref=pair_in.at[n], send_sem=pair_send.at[n], recv_sem=pair_recv.at[n],
            device_id=(g, target), device_id_type=MESH,
        )

    def half(n):
        return pltpu.make_async_remote_copy(
            src_ref=half_out.at[n], dst_ref=half_in.at[n], send_sem=half_send.at[n], recv_sem=half_recv.at[n],
            device_id=(g, d + 1 - 2 * core), device_id_type=MESH,
        )

    def part(n, j):
        return pltpu.make_async_remote_copy(
            src_ref=part_out.at[n, j], dst_ref=part_in.at[n, chip], send_sem=part_send.at[n, j],
            recv_sem=part_recv.at[n, chip], device_id=(g, 2 * j + core), device_id_type=MESH,
        )

    def part_arrival(n, j):
        return pltpu.make_async_remote_copy(
            src_ref=part_out.at[n, j], dst_ref=part_in.at[n, j], send_sem=part_send.at[n, j],
            recv_sem=part_recv.at[n, j], device_id=(g, 2 * j + core), device_id_type=MESH,
        )

    def part_first(n, c, z, target):
        return pltpu.make_async_remote_copy(
            src_ref=part_out.at[n, 0], dst_ref=first_in.at[n, c, z], send_sem=part_send.at[n, 0],
            recv_sem=first_recv.at[n, c, z], device_id=(g, target), device_id_type=MESH,
        )

    def chunk(n, c, z, target):
        return pltpu.make_async_remote_copy(
            src_ref=chunk_out.at[n], dst_ref=chunk_in.at[n, c, z], send_sem=chunk_send.at[n],
            recv_sem=chunk_recv.at[n, c, z], device_id=(g, target), device_id_type=MESH,
        )

    def cast(n, k, j, slot):
        rows = pl.ds(k * SLAB, SLAB)
        return pltpu.make_async_remote_copy(
            src_ref=currents.at[n, rows], dst_ref=currents.at[n, rows], send_sem=cast_send.at[n, slot],
            recv_sem=cast_recv.at[n, k], device_id=(g, 2 * j), device_id_type=MESH,
        )

    def fan(n, k, target):
        rows = pl.ds(k * SLAB, SLAB)
        return pltpu.make_async_remote_copy(
            src_ref=currents.at[n, rows], dst_ref=currents.at[n, rows], send_sem=fan_send.at[n, k],
            recv_sem=fan_recv.at[n, k], device_id=(g, target), device_id_type=MESH,
        )

    def cast_all(n, j):
        return pltpu.make_async_remote_copy(
            src_ref=currents.at[n], dst_ref=currents.at[n], send_sem=cast_send.at[n, j],
            recv_sem=cast_recv.at[n, 0], device_id=(g, 2 * j), device_id_type=MESH,
        )

    def fan_all(n, target):
        return pltpu.make_async_remote_copy(
            src_ref=currents.at[n], dst_ref=currents.at[n], send_sem=fan_send.at[n, 0],
            recv_sem=fan_recv.at[n, 0], device_id=(g, target), device_id_type=MESH,
        )

    def store(n):
        return pltpu.make_async_copy(currents.at[n], out_hbm.at[n], out_sem.at[n])

    local[0].wait()
    pack(0)
    enter()
    for dx, dy in OFFSETS:
        block_copy(0, dx, dy).start()
    start_shift(0)

    weights[GROUPS * PLACES] = jnp.zeros((BLK, BLK), weights.dtype)
    for i in range(SIDE * 2):
        rows = jnp.broadcast_to(diag_ref[i : i + 1, :], (COLS, COLS))
        rdiag[pl.ds(i * COLS, COLS), :] = 1.0 / jnp.transpose(rows)
    local[1].wait()

    def spread(hx, carry):
        for hy in range(SIDE):
            h = hx * SIDE + hy
            for r in range(SIDE):
                place = jnp.int32(GROUPS * PLACES)
                for l in range(PLACES):
                    hit = jnp.logical_and(row_ref[l, 0, h] == r, l < count_ref[h])
                    place = jnp.where(hit, h * PLACES + l, place)
                dense[hx, pl.ds(r * BLK, BLK), pl.ds(hy * BLK, BLK)] = weights[place]
        return carry

    lax.fori_loop(0, SIDE, spread, 0)
    local[2].wait()
    local[3].wait()

    def fold_sweeps():
        wide = 2 * COLS

        def scaled(t, half):
            tile = pl.ds(pl.multiple_of(t * wide + half * COLS, COLS), COLS)
            return tile, self_block[:, tile].astype(jnp.float32) * rdiag[...]

        def scale(t, carry):
            for half in range(2):
                tile, value = scaled(t, half)
                ratio[:, tile] = value.astype(jnp.bfloat16)
            return carry

        lax.fori_loop(0, ROWS // wide, scale, 0)

        def fold(factor, result):
            def body(t, carry):
                both = pl.ds(pl.multiple_of(t * wide, wide), wide)
                product = jnp.dot(ratio[...], factor[:, both], preferred_element_type=jnp.float32)
                for half in range(2):
                    tile, value = scaled(t, half)
                    part = product[:, half * COLS : half * COLS + COLS]
                    result[:, tile] = (value - part).astype(jnp.bfloat16)
                return carry

            lax.fori_loop(0, ROWS // wide, body, 0)

        fold(ratio, power)
        fold(power, self_block)

    last = STEPS - 1

    def step(n, carry):
        def quarter(c, carry):
            hx = (x + jnp.where(c == 0, 2, jnp.where(c == 1, 3, jnp.where(c == 2, 1, 0)))) % SIDE
            for hy in range(SIDE):
                @pl.when(jnp.logical_not(jnp.logical_and(hx == x, hy == y)))
                def _():
                    block_arrival(n, hx, hy).wait_recv()

            @pl.when(jnp.logical_and(c == 0, jnp.logical_and(first, jnp.logical_or(n == 1, n == 2))))
            def _():
                pl.semaphore_signal(turn_sem, inc=1, device_id=(g, 1), device_id_type=MESH)

            @pl.when(c == 1)
            def _():
                @pl.when(jnp.logical_and(d > n, n < STEPS - 1))
                def _():
                    shift_in = pltpu.make_async_remote_copy(
                        src_ref=held.at[n], dst_ref=held.at[n + 1], send_sem=shift_send.at[n],
                        recv_sem=shift_recv.at[n + 1], device_id=(g, d - 1), device_id_type=MESH,
                    )
                    shift_in.wait_recv()
                    start_shift(n + 1)
                    send_blocks(n + 1)

            value = jnp.dot(
                dense[hx], blocks[n, hx].reshape(ROWS, COLS), preferred_element_type=jnp.float32
            )

            @pl.when(c == 0)
            def _():
                total[...] = value

            @pl.when(c > 0)
            def _():
                total[...] += value

            return carry

        lax.fori_loop(0, SIDE, quarter, 0)

        @pl.when(d == 1)
        def _():
            pair_out[n] = total[...].astype(jnp.bfloat16)
            pair(n, 0).start()

        @pl.when(d > 1)
        def _():
            mine = pl.ds(pl.multiple_of(core * HALF, HALF), HALF)
            other = pl.ds(pl.multiple_of(HALF - core * HALF, HALF), HALF)
            half_out[n] = total[other, :].astype(jnp.bfloat16)
            half(n).start()
            half(n).wait_recv()
            summed = total[mine, :] + half_in[n].astype(jnp.float32)
            total[mine, :] = summed
            part_out[n] = summed.astype(jnp.bfloat16).reshape(CHIPS, PART, COLS)
            for j in (4, 3, 5, 2, 6, 1, 7):
                @pl.when(j != chip)
                def _():
                    part(n, j).start()
            part_first(n, core, chip, 0).start()

            @pl.when(jnp.logical_and(d == 2, n == 2))
            def _():
                cast_all(0, 0).wait_recv()
                held[n + 1] = currents[0].reshape(SIDE, BLK, COLS)
                send_blocks(n + 1)

            place = pl.ds(pl.multiple_of(core * HALF + chip * PART, PART), PART)
            part_in[n, chip] = jnp.zeros((PART, COLS), jnp.bfloat16)
            for j in range(1, CHIPS):
                @pl.when(j != chip)
                def _():
                    part_arrival(n, j).wait_recv()
            value = total[place, :]
            for j in range(1, CHIPS):
                value += part_in[n, j].astype(jnp.float32)
            chunk_out[n] = value.astype(jnp.bfloat16)
            chunk(n, core, chip, 0).start()

        @pl.when(first)
        def _():
            pl.when(n == 0)(fold_sweeps)

            def arrive(z, carry):
                for c in range(2):
                    part_first(n, c, z, 2).wait_recv()
                    chunk(n, c, z, 2).wait_recv()
                return carry

            lax.fori_loop(1, CHIPS, arrive, 0)
            for c in range(2):
                value = first_in[n, c, 1].astype(jnp.float32)
                for z in range(2, CHIPS):
                    value += first_in[n, c, z].astype(jnp.float32)
                chunk_in[n, c, 0] = value.astype(jnp.bfloat16)
            pair(n, 1).wait_recv()
            value = incident[n].astype(jnp.float32) - chunk_in[n].reshape(ROWS, COLS).astype(jnp.float32)
            value = (value - pair_in[n].astype(jnp.float32) - total[...]) * rdiag[...]
            total[...] = value
            coupled = jnp.dot(self_block[...], value.astype(jnp.bfloat16), preferred_element_type=jnp.float32)
            current = (total[...] - coupled).astype(jnp.bfloat16)
            currents[n] = current

            @pl.when(n < STEPS - 1)
            def _():
                held[n + 1] = current.reshape(SIDE, BLK, COLS)
                send_blocks(n + 1)
                fan_all(n, 1).start()
                for j in (1, 4, 3, 5, 2, 6, 7):
                    cast_all(n, j).start()

            @pl.when(n == last)
            def _():
                for j in (4, 3, 5, 2, 6, 1, 7):
                    cast(last, j, j, j).start()
                for j in (4, 3, 5, 2, 6, 1, 7):
                    cast(last, 0, j, CHIPS + j).start()
                for k in range(CHIPS):
                    fan(last, k, 1).start()

            store(n).start()

        @pl.when(jnp.logical_and(d == 1, jnp.logical_or(n == 1, n == 2)))
        def _():
            fan_all(n - 1, 0).wait_recv()
            held[n + 1] = currents[n - 1].reshape(SIDE, BLK, COLS)
            pack(n + 1)
            pl.semaphore_wait(turn_sem, 1)
            for dx, dy in OFFSETS:
                block_copy(n + 1, dx, dy).start()

        return carry

    lax.fori_loop(0, STEPS, step, 0)

    def finish(n, carry):
        @pl.when(jnp.logical_and(core == 0, d > 0))
        def _():
            @pl.when(jnp.logical_not(jnp.logical_and(d == 2, n == 0)))
            def _():
                cast_all(n, 0).wait_recv()

            fan_all(n, d + 1).start()
            store(n).start()

        @pl.when(core == 1)
        def _():
            @pl.when(jnp.logical_or(d > 1, n == last - 1))
            def _():
                fan_all(n, d - 1).wait_recv()

            store(n).start()

        return carry

    lax.fori_loop(0, last, finish, 0)

    @pl.when(jnp.logical_and(core == 0, d > 0))
    def _():
        cast(last, chip, 0, 0).wait_recv()
        for j in range(1, CHIPS):
            to = (chip + j) % CHIPS

            @pl.when(to > 0)
            def _():
                cast(last, chip, to, to).start()
        fan(last, chip, d + 1).start()
        for j in range(1, CHIPS):
            k = (chip + j) % CHIPS
            cast(last, k, 0, 0).wait_recv()
            fan(last, k, d + 1).start()
        store(last).start()

    @pl.when(core == 1)
    def _():
        for k in range(CHIPS):
            fan(last, k, d - 1).wait_recv()
        store(last).start()

    def drain(n, carry):
        for dx, dy in OFFSETS:
            block_copy(n, dx, dy).wait_send()

        @pl.when(jnp.logical_and(n < STEPS - 1, jnp.logical_and(d >= n, d < DELAYS - 1)))
        def _():
            shift(n).wait_send()

        @pl.when(d == 1)
        def _():
            pair(n, 0).wait_send()

        @pl.when(d > 1)
        def _():
            half(n).wait_send()
            part_first(n, core, chip, 0).wait_send()
            chunk(n, core, chip, 0).wait_send()
            for j in range(1, CHIPS):
                @pl.when(j != chip)
                def _():
                    part(n, j).wait_send()

        @pl.when(jnp.logical_and(core == 0, n < last))
        def _():
            fan_all(n, d + 1).wait_send()

        @pl.when(jnp.logical_and(first, n < last))
        def _():
            for j in range(1, CHIPS):
                cast_all(n, j).wait_send()

        store(n).wait()
        return carry

    lax.fori_loop(0, STEPS, drain, 0)

    @pl.when(core == 0)
    def _():
        for k in range(CHIPS):
            fan(last, k, d + 1).wait_send()
        for j in range(1, CHIPS):
            @pl.when(j != chip)
            def _():
                cast(last, chip, j, j).wait_send()

    @pl.when(first)
    def _():
        for j in range(1, CHIPS):
            cast(last, 0, j, CHIPS + j).wait_send()


def local(retarded, block_row, block_count, send_pick, history, incident, self_block, sheet_diag):
    smem = pl.BlockSpec(memory_space=pltpu.SMEM)
    vmem = pl.BlockSpec(memory_space=pltpu.VMEM)
    hbm = pl.BlockSpec(memory_space=pl.ANY)
    bf16, f32 = jnp.bfloat16, jnp.float32
    dma = pltpu.SemaphoreType.DMA
    call = pl.pallas_call(
        kernel,
        out_shape=jax.ShapeDtypeStruct((STEPS, ROWS, COLS), bf16),
        in_specs=[smem, smem, smem, hbm, hbm, hbm, hbm, vmem],
        out_specs=hbm,
        scratch_shapes=[
            pltpu.VMEM((GROUPS * PLACES + 1, BLK, BLK), bf16),
            pltpu.VMEM((SIDE, ROWS, ROWS), bf16),
            pltpu.VMEM((ROWS, ROWS), bf16),
            pltpu.VMEM((ROWS, ROWS), bf16),
            pltpu.VMEM((ROWS, ROWS), bf16),
            pltpu.VMEM((STEPS, ROWS, COLS), bf16),
            pltpu.VMEM((STEPS, SIDE, BLK, COLS), bf16),
            pltpu.VMEM((SIDE, BLK, COLS), bf16),
            pltpu.VMEM((STEPS, GROUPS, BLK, COLS), bf16),
            pltpu.VMEM((STEPS, SIDE, SIDE, BLK, COLS), bf16),
            pltpu.VMEM((ROWS, COLS), f32),
            pltpu.VMEM((ROWS, COLS), f32),
            pltpu.VMEM((STEPS, ROWS, COLS), bf16),
            pltpu.VMEM((STEPS, ROWS, COLS), bf16),
            pltpu.VMEM((STEPS, HALF, COLS), bf16),
            pltpu.VMEM((STEPS, HALF, COLS), bf16),
            pltpu.VMEM((STEPS, CHIPS, PART, COLS), bf16),
            pltpu.VMEM((STEPS, CHIPS, PART, COLS), bf16),
            pltpu.VMEM((STEPS, PART, COLS), bf16),
            pltpu.VMEM((STEPS, 2, CHIPS, PART, COLS), bf16),
            pltpu.VMEM((STEPS, 2, CHIPS, PART, COLS), bf16),
            pltpu.VMEM((STEPS, ROWS, COLS), bf16),
            dma((4,)),
            dma((STEPS, GROUPS)), dma((STEPS, GROUPS)),
            dma((STEPS,)), dma((STEPS,)),
            dma((STEPS,)), dma((STEPS,)),
            dma((STEPS,)), dma((STEPS,)),
            dma((STEPS, CHIPS)), dma((STEPS, CHIPS)),
            dma((STEPS,)), dma((STEPS, 2, CHIPS)), dma((STEPS, 2, CHIPS)),
            dma((STEPS, 2 * CHIPS)), dma((STEPS, CHIPS)),
            dma((STEPS, CHIPS)), dma((STEPS, CHIPS)),
            dma((STEPS,)),
            pltpu.SemaphoreType.REGULAR,
        ],
        compiler_params=pltpu.CompilerParams(
            collective_id=0, has_side_effects=True, vmem_limit_bytes=56 * 2**20
        ),
        cost_estimate=pl.CostEstimate(flops=8 * 10**9, bytes_accessed=12 * 10**6, transcendentals=0),
    )
    return call(
        jnp.transpose(block_row, (2, 0, 1)), block_count[0], send_pick[0],
        retarded.reshape(GROUPS * PLACES, BLK, BLK), history.reshape(SIDE, BLK, COLS),
        incident, self_block, sheet_diag.reshape(SIDE * 2, COLS),
    )


def solution(mesh):
    placed = (
        P("delay", "group", None, None, None),
        P("delay", "group", None),
        P("delay", "group"),
        P("delay", None, None),
        P("delay", "group", None),
        P(None, "group", None),
        P("group", None),
        P("group"),
    )
    return jax.shard_map(
        local, mesh=mesh, in_specs=placed, out_specs=P(None, "group", None), check_vma=False
    )
```

time: 119 us -> 99.2 us (0.83)
  Pallas kernels: 116 us -> 96.8 us
  local copies, waits for them, and re-layouts: 3.62 us -> 2.26 us
    pallas_call x1, Pallas kernels: 116 us -> 96.8 us  [local(): call(jnp.transpose(block_row, (2, 0, 1)), block_count[0], send_pick[0], r...]
    squeeze x1 -> x0, local copies, waits for them, and re-layouts: 1.35 us -> none  [local(): block_row[0]]
where the time goes in v2:
time: 99.2 us; the launch traced here: 99 us
  Pallas kernels  96.8 us (98%)
  local copies, waits for them, and re-layouts  2.26 us (2%)
    pallas_call x1, Pallas kernels, local(): call(jnp.transpose(block_row, (2, 0, 1)), block_count[0], send_pick[0], r...  96.8 us
    unnamed x1, local copies, waits for them, and re-layouts  2.26 us

profile of v2, /device:TPU:33, one launch (start us, length us, event | category | flops | bytes accessed | tf_op | source)
XLA Modules:
  0.0 99.0 jit_solution(773827251299075800)
XLA Ops:
  0.0 96.8 %shard_map.82 = bf16[4,1024,128]{2,1,0:T(8,128)(2,1)} custom-call(s32[3,1,16]{2,1,0:T(1,128)} %bitcast.10, s32[16]{0:T(128)} %bitcast.11, s32[16,16]{1,0:T(8,128)} %bitcast.8, bf16[48,256,256]{2,1,0:T(8,128)(2,1)} %bitcast.6, bf16[4,256,128]{2,1,0:T(8,128)(2,1)} %bitcast.7, bf16[4,1024,128]{2,1,0:T(8,128)(2,1)} %incident_hbm.1, bf16[1024,1024]{1,0:T(8,128)(2,1)} %self_hbm.1, ...), custom_call_target="tpu_custom_call" | custom-call | flops 8000000000 | bytes 12000000 | tf_op jit(solution)/shard_map/pallas_call | solution.py:529
  96.8 2.3 %copy.10 = bf16[4,1024,128]{2,1,0:T(8,128)(2,1)} copy(bf16[4,1024,128]{2,1,0:T(8,128)(2,1)} %shard_map.82) | data formatting | bytes 2097152

commit v3 on v2

--- a/solution.py
+++ b/solution.py
@@ -89,16 +89,19 @@
         h = peer(dx, dy)
         return pltpu.make_async_remote_copy(
             src_ref=staged.at[n, h], dst_ref=blocks.at[n, x, y],
-            send_sem=block_send.at[n, h], recv_sem=block_recv.at[n, g],
+            send_sem=block_send.at[n], recv_sem=block_recv.at[n, x],
             device_id=(h, d), device_id_type=MESH,
         )
 
-    def block_arrival(n, hx, hy):
-        return pltpu.make_async_remote_copy(
-            src_ref=staged.at[n, 0], dst_ref=blocks.at[n, hx, hy],
-            send_sem=block_send.at[n, 0], recv_sem=block_recv.at[n, hx * SIDE + hy],
-            device_id=(peer(1, 0), d), device_id_type=MESH,
-        )
+    def all_sent(ref, sem):
+        pltpu.make_async_remote_copy(
+            src_ref=ref, dst_ref=ref, send_sem=sem, recv_sem=sem, device_id=(g, d + 1 - 2 * core), device_id_type=MESH,
+        ).wait_send()
+
+    def all_come(ref, sem):
+        pltpu.make_async_remote_copy(
+            src_ref=ref, dst_ref=ref, send_sem=sem, recv_sem=sem, device_id=(g, d + 1 - 2 * core), device_id_type=MESH,
+        ).wait_recv()
 
     def pack(n):
         source[...] = held[n]
@@ -122,68 +125,64 @@
 
     def pair(n, target):
         return pltpu.make_async_remote_copy(
-            src_ref=pair_out.at[n], dst_ref=pair_in.at[n], send_sem=pair_send.at[n], recv_sem=pair_recv.at[n],
+            src_ref=pair_out.at[n], dst_ref=pair_in.at[n], send_sem=pair_send.at[0], recv_sem=pair_recv.at[n],
             device_id=(g, target), device_id_type=MESH,
         )
 
     def half(n):
         return pltpu.make_async_remote_copy(
-            src_ref=half_out.at[n], dst_ref=half_in.at[n], send_sem=half_send.at[n], recv_sem=half_recv.at[n],
+            src_ref=half_out.at[n], dst_ref=half_in.at[n], send_sem=half_send.at[0], recv_sem=half_recv.at[n],
             device_id=(g, d + 1 - 2 * core), device_id_type=MESH,
         )
 
     def part(n, j):
         return pltpu.make_async_remote_copy(
-            src_ref=part_out.at[n, j], dst_ref=part_in.at[n, chip], send_sem=part_send.at[n, j],
-            recv_sem=part_recv.at[n, chip], device_id=(g, 2 * j + core), device_id_type=MESH,
-        )
-
-    def part_arrival(n, j):
-        return pltpu.make_async_remote_copy(
-            src_ref=part_out.at[n, j], dst_ref=part_in.at[n, j], send_sem=part_send.at[n, j],
-            recv_sem=part_recv.at[n, j], device_id=(g, 2 * j + core), device_id_type=MESH,
+            src_ref=part_out.at[n, j], dst_ref=part_in.at[n, chip], send_sem=part_send.at[n],
+            recv_sem=part_recv.at[n], device_id=(g, 2 * j + core), device_id_type=MESH,
         )
 
     def part_first(n, c, z, target):
         return pltpu.make_async_remote_copy(
-            src_ref=part_out.at[n, 0], dst_ref=first_in.at[n, c, z], send_sem=part_send.at[n, 0],
-            recv_sem=first_recv.at[n, c, z], device_id=(g, target), device_id_type=MESH,
+            src_ref=part_out.at[n, 0], dst_ref=first_in.at[n, c, z], send_sem=part_send.at[n],
+            recv_sem=first_recv.at[n], device_id=(g, target), device_id_type=MESH,
         )
 
     def chunk(n, c, z, target):
         return pltpu.make_async_remote_copy(
-            src_ref=chunk_out.at[n], dst_ref=chunk_in.at[n, c, z], send_sem=chunk_send.at[n],
-            recv_sem=chunk_recv.at[n, c, z], device_id=(g, target), device_id_type=MESH,
-        )
-
-    def cast(n, k, j, slot):
+            src_ref=chunk_out.at[n], dst_ref=chunk_in.at[n, c, z], send_sem=chunk_send.at[0],
+            recv_sem=chunk_recv.at[n], device_id=(g, target), device_id_type=MESH,
+        )
+
+    last = STEPS - 1
+
+    def cast(k, j):
         rows = pl.ds(k * SLAB, SLAB)
         return pltpu.make_async_remote_copy(
-            src_ref=currents.at[n, rows], dst_ref=currents.at[n, rows], send_sem=cast_send.at[n, slot],
-            recv_sem=cast_recv.at[n, k], device_id=(g, 2 * j), device_id_type=MESH,
-        )
-
-    def fan(n, k, target):
+            src_ref=currents.at[last, rows], dst_ref=currents.at[last, rows], send_sem=cast_send.at[last],
+            recv_sem=cast_recv.at[last + k], device_id=(g, 2 * j), device_id_type=MESH,
+        )
+
+    def fan(k, target):
         rows = pl.ds(k * SLAB, SLAB)
         return pltpu.make_async_remote_copy(
-            src_ref=currents.at[n, rows], dst_ref=currents.at[n, rows], send_sem=fan_send.at[n, k],
-            recv_sem=fan_recv.at[n, k], device_id=(g, target), device_id_type=MESH,
+            src_ref=currents.at[last, rows], dst_ref=currents.at[last, rows], send_sem=fan_send.at[last],
+            recv_sem=fan_recv.at[last], device_id=(g, target), device_id_type=MESH,
         )
 
     def cast_all(n, j):
         return pltpu.make_async_remote_copy(
-            src_ref=currents.at[n], dst_ref=currents.at[n], send_sem=cast_send.at[n, j],
-            recv_sem=cast_recv.at[n, 0], device_id=(g, 2 * j), device_id_type=MESH,
+            src_ref=currents.at[n], dst_ref=currents.at[n], send_sem=cast_send.at[n],
+            recv_sem=cast_recv.at[n], device_id=(g, 2 * j), device_id_type=MESH,
         )
 
     def fan_all(n, target):
         return pltpu.make_async_remote_copy(
-            src_ref=currents.at[n], dst_ref=currents.at[n], send_sem=fan_send.at[n, 0],
-            recv_sem=fan_recv.at[n, 0], device_id=(g, target), device_id_type=MESH,
+            src_ref=currents.at[n], dst_ref=currents.at[n], send_sem=fan_send.at[n],
+            recv_sem=fan_recv.at[n], device_id=(g, target), device_id_type=MESH,
         )
 
     def store(n):
-        return pltpu.make_async_copy(currents.at[n], out_hbm.at[n], out_sem.at[n])
+        return pltpu.make_async_copy(currents.at[n], out_hbm.at[n], out_sem.at[0])
 
     local[0].wait()
     pack(0)
@@ -243,15 +242,16 @@
         fold(ratio, power)
         fold(power, self_block)
 
-    last = STEPS - 1
-
     def step(n, carry):
         def quarter(c, carry):
             hx = (x + jnp.where(c == 0, 2, jnp.where(c == 1, 3, jnp.where(c == 2, 1, 0)))) % SIDE
-            for hy in range(SIDE):
-                @pl.when(jnp.logical_not(jnp.logical_and(hx == x, hy == y)))
-                def _():
-                    block_arrival(n, hx, hy).wait_recv()
+            @pl.when(hx == x)
+            def _():
+                all_come(blocks.at[n, hx, pl.ds(0, SIDE - 1)], block_recv.at[n, hx])
+
+            @pl.when(hx != x)
+            def _():
+                all_come(blocks.at[n, hx], block_recv.at[n, hx])
 
             @pl.when(jnp.logical_and(c == 0, jnp.logical_and(first, jnp.logical_or(n == 1, n == 2))))
             def _():
@@ -313,11 +313,8 @@
                 send_blocks(n + 1)
 
             place = pl.ds(pl.multiple_of(core * HALF + chip * PART, PART), PART)
+            all_come(part_in.at[n, pl.ds(0, CHIPS - 2)], part_recv.at[n])
             part_in[n, chip] = jnp.zeros((PART, COLS), jnp.bfloat16)
-            for j in range(1, CHIPS):
-                @pl.when(j != chip)
-                def _():
-                    part_arrival(n, j).wait_recv()
             value = total[place, :]
             for j in range(1, CHIPS):
                 value += part_in[n, j].astype(jnp.float32)
@@ -328,13 +325,8 @@
         def _():
             pl.when(n == 0)(fold_sweeps)
 
-            def arrive(z, carry):
-                for c in range(2):
-                    part_first(n, c, z, 2).wait_recv()
-                    chunk(n, c, z, 2).wait_recv()
-                return carry
-
-            lax.fori_loop(1, CHIPS, arrive, 0)
+            all_come(first_in.at[n, :, pl.ds(0, CHIPS - 1)], first_recv.at[n])
+            all_come(chunk_in.at[n, :, pl.ds(0, CHIPS - 1)], chunk_recv.at[n])
             for c in range(2):
                 value = first_in[n, c, 1].astype(jnp.float32)
                 for z in range(2, CHIPS):
@@ -359,11 +351,11 @@
             @pl.when(n == last)
             def _():
                 for j in (4, 3, 5, 2, 6, 1, 7):
-                    cast(last, j, j, j).start()
+                    cast(j, j).start()
                 for j in (4, 3, 5, 2, 6, 1, 7):
-                    cast(last, 0, j, CHIPS + j).start()
+                    cast(0, j).start()
                 for k in range(CHIPS):
-                    fan(last, k, 1).start()
+                    fan(k, 1).start()
 
             store(n).start()
 
@@ -404,75 +396,66 @@
 
     @pl.when(jnp.logical_and(core == 0, d > 0))
     def _():
-        cast(last, chip, 0, 0).wait_recv()
+        cast(chip, 0).wait_recv()
         for j in range(1, CHIPS):
             to = (chip + j) % CHIPS
 
             @pl.when(to > 0)
             def _():
-                cast(last, chip, to, to).start()
-        fan(last, chip, d + 1).start()
+                cast(chip, to).start()
+        fan(chip, d + 1).start()
         for j in range(1, CHIPS):
             k = (chip + j) % CHIPS
-            cast(last, k, 0, 0).wait_recv()
-            fan(last, k, d + 1).start()
+            cast(k, 0).wait_recv()
+            fan(k, d + 1).start()
         store(last).start()
 
     @pl.when(core == 1)
     def _():
-        for k in range(CHIPS):
-            fan(last, k, d - 1).wait_recv()
+        all_come(currents.at[last], fan_recv.at[last])
         store(last).start()
 
     def drain(n, carry):
-        for dx, dy in OFFSETS:
-            block_copy(n, dx, dy).wait_send()
+        all_sent(staged.at[n, pl.ds(0, GROUPS - 1)], block_send.at[n])
 
         @pl.when(jnp.logical_and(n < STEPS - 1, jnp.logical_and(d >= n, d < DELAYS - 1)))
         def _():
             shift(n).wait_send()
 
-        @pl.when(d == 1)
-        def _():
-            pair(n, 0).wait_send()
-
         @pl.when(d > 1)
         def _():
-            half(n).wait_send()
-            part_first(n, core, chip, 0).wait_send()
-            chunk(n, core, chip, 0).wait_send()
-            for j in range(1, CHIPS):
-                @pl.when(j != chip)
-                def _():
-                    part(n, j).wait_send()
-
-        @pl.when(jnp.logical_and(core == 0, n < last))
-        def _():
-            fan_all(n, d + 1).wait_send()
+            all_sent(part_out.at[n, pl.ds(0, CHIPS - 1)], part_send.at[n])
+
+        @pl.when(core == 0)
+        def _():
+            all_sent(currents.at[n], fan_send.at[n])
 
         @pl.when(jnp.logical_and(first, n < last))
         def _():
-            for j in range(1, CHIPS):
-                cast_all(n, j).wait_send()
-
-        store(n).wait()
+            all_sent(weights.at[pl.ds(0, 2 * CHIPS - 2)], cast_send.at[n])
+
         return carry
 
     lax.fori_loop(0, STEPS, drain, 0)
 
-    @pl.when(core == 0)
-    def _():
-        for k in range(CHIPS):
-            fan(last, k, d + 1).wait_send()
-        for j in range(1, CHIPS):
-            @pl.when(j != chip)
-            def _():
-                cast(last, chip, j, j).wait_send()
+    @pl.when(d == 1)
+    def _():
+        all_sent(pair_out, pair_send.at[0])
+
+    @pl.when(d > 1)
+    def _():
+        all_sent(half_out, half_send.at[0])
+        all_sent(chunk_out, chunk_send.at[0])
 
     @pl.when(first)
     def _():
-        for j in range(1, CHIPS):
-            cast(last, 0, j, CHIPS + j).wait_send()
+        all_sent(staged.at[0, pl.ds(0, CHIPS - 1)], cast_send.at[last])
+
+    @pl.when(jnp.logical_and(core == 0, d > 0))
+    def _():
+        all_sent(staged.at[0, pl.ds(0, CHIPS // 2 - 1)], cast_send.at[last])
+
+    pltpu.make_async_copy(currents, out_hbm, out_sem.at[0]).wait()
 
 
 def local(retarded, block_row, block_count, send_pick, history, incident, self_block, sheet_diag):
@@ -510,15 +493,15 @@
             pltpu.VMEM((STEPS, 2, CHIPS, PART, COLS), bf16),
             pltpu.VMEM((STEPS, ROWS, COLS), bf16),
             dma((4,)),
-            dma((STEPS, GROUPS)), dma((STEPS, GROUPS)),
+            dma((STEPS,)), dma((STEPS, SIDE)),
             dma((STEPS,)), dma((STEPS,)),
+            dma((1,)), dma((STEPS,)),
+            dma((1,)), dma((STEPS,)),
             dma((STEPS,)), dma((STEPS,)),
+            dma((1,)), dma((STEPS,)), dma((STEPS,)),
+            dma((STEPS,)), dma((STEPS + CHIPS,)),
             dma((STEPS,)), dma((STEPS,)),
-            dma((STEPS, CHIPS)), dma((STEPS, CHIPS)),
-            dma((STEPS,)), dma((STEPS, 2, CHIPS)), dma((STEPS, 2, CHIPS)),
-            dma((STEPS, 2 * CHIPS)), dma((STEPS, CHIPS)),
-            dma((STEPS, CHIPS)), dma((STEPS, CHIPS)),
-            dma((STEPS,)),
+            dma((1,)),
             pltpu.SemaphoreType.REGULAR,
         ],
         compiler_params=pltpu.CompilerParams(

time: 99.2 us -> 95.2 us (0.960)
  Pallas kernels: 96.8 us -> 92.7 us
    pallas_call x1, Pallas kernels: 96.8 us -> 92.7 us  [local(): call(jnp.transpose(block_row, (2, 0, 1)), block_count[0], send_pick[0], r...]
where the time goes in v3:
time: 95.2 us; the launch traced here: 95 us
  Pallas kernels  92.7 us (97%)
  local copies, waits for them, and re-layouts  2.26 us (2%)
    pallas_call x1, Pallas kernels, local(): call(jnp.transpose(block_row, (2, 0, 1)), block_count[0], send_pick[0], r...  92.7 us
    unnamed x1, local copies, waits for them, and re-layouts  2.26 us

profile of v3, /device:TPU:33, one launch (start us, length us, event | category | flops | bytes accessed | tf_op | source)
XLA Modules:
  0.0 95.0 jit_solution(9510589154999748456)
XLA Ops:
  0.0 92.7 %shard_map.82 = bf16[4,1024,128]{2,1,0:T(8,128)(2,1)} custom-call(s32[3,1,16]{2,1,0:T(1,128)} %bitcast.10, s32[16]{0:T(128)} %bitcast.11, s32[16,16]{1,0:T(8,128)} %bitcast.8, bf16[48,256,256]{2,1,0:T(8,128)(2,1)} %bitcast.6, bf16[4,256,128]{2,1,0:T(8,128)(2,1)} %bitcast.7, bf16[4,1024,128]{2,1,0:T(8,128)(2,1)} %incident_hbm.1, bf16[1024,1024]{1,0:T(8,128)(2,1)} %self_hbm.1, ...), custom_call_target="tpu_custom_call" | custom-call | flops 8000000000 | bytes 12000000 | tf_op jit(solution)/shard_map/pallas_call | solution.py:512
  92.7 2.3 %copy.10 = bf16[4,1024,128]{2,1,0:T(8,128)(2,1)} copy(bf16[4,1024,128]{2,1,0:T(8,128)(2,1)} %shard_map.82) | data formatting | bytes 2097152

commit v4 on v3

--- a/solution.py
+++ b/solution.py
@@ -169,6 +169,10 @@
             recv_sem=fan_recv.at[last], device_id=(g, target), device_id_type=MESH,
         )
 
+    def store_slab(k):
+        rows = pl.ds(k * SLAB, SLAB)
+        return pltpu.make_async_copy(currents.at[last, rows], out_hbm.at[last, rows], out_sem.at[0])
+
     def cast_all(n, j):
         return pltpu.make_async_remote_copy(
             src_ref=currents.at[n], dst_ref=currents.at[n], send_sem=cast_send.at[n],
@@ -397,18 +401,19 @@
     @pl.when(jnp.logical_and(core == 0, d > 0))
     def _():
         cast(chip, 0).wait_recv()
-        for j in range(1, CHIPS):
+        for j in (4, 3, 5, 2, 6, 1, 7):
             to = (chip + j) % CHIPS
 
             @pl.when(to > 0)
             def _():
                 cast(chip, to).start()
         fan(chip, d + 1).start()
+        store_slab(chip).start()
         for j in range(1, CHIPS):
             k = (chip + j) % CHIPS
             cast(k, 0).wait_recv()
             fan(k, d + 1).start()
-        store(last).start()
+            store_slab(k).start()
 
     @pl.when(core == 1)
     def _():

time: 95.2 us -> 95.2 us (level)
  no operation moved by 1% of the time
where the time goes in v4:
time: 95.2 us; the launch traced here: 95 us
  Pallas kernels  92.7 us (97%)
  local copies, waits for them, and re-layouts  2.26 us (2%)
    pallas_call x1, Pallas kernels, local(): call(jnp.transpose(block_row, (2, 0, 1)), block_count[0], send_pick[0], r...  92.7 us
    unnamed x1, local copies, waits for them, and re-layouts  2.26 us

profile of v4, /device:TPU:33, one launch (start us, length us, event | category | flops | bytes accessed | tf_op | source)
XLA Modules:
  0.0 95.0 jit_solution(86443274368739293)
XLA Ops:
  0.0 92.7 %shard_map.82 = bf16[4,1024,128]{2,1,0:T(8,128)(2,1)} custom-call(s32[3,1,16]{2,1,0:T(1,128)} %bitcast.10, s32[16]{0:T(128)} %bitcast.11, s32[16,16]{1,0:T(8,128)} %bitcast.8, bf16[48,256,256]{2,1,0:T(8,128)(2,1)} %bitcast.6, bf16[4,256,128]{2,1,0:T(8,128)(2,1)} %bitcast.7, bf16[4,1024,128]{2,1,0:T(8,128)(2,1)} %incident_hbm.1, bf16[1024,1024]{1,0:T(8,128)(2,1)} %self_hbm.1, ...), custom_call_target="tpu_custom_call" | custom-call | flops 8000000000 | bytes 12000000 | tf_op jit(solution)/shard_map/pallas_call | solution.py:517
  92.7 2.3 %copy.10 = bf16[4,1024,128]{2,1,0:T(8,128)(2,1)} copy(bf16[4,1024,128]{2,1,0:T(8,128)(2,1)} %shard_map.82) | data formatting | bytes 2097152
